TPU v7x, 32 devices: a whole 2x2x4 slice. The times are simulated.
32 devices in a mesh: dp: 8 (over y, x, core), tensor: 4 (over z).
Axes of the slice: x: 2, y: 2, z: 4, core: 2. Of those that a mesh axis runs over, the one named last changes fastest.
Arguments:
- block_input: bfloat16 [8192, 1536], P(('dp', 'tensor')), may hold values from -6 to 6
- attn_gain: bfloat16 [1536], P('dp'), may hold values from 0.5 to 1.5
- w_query: bfloat16 [1536, 1536], P('dp', 'tensor'), may hold values from -0.15625 to 0.15625
- w_key: bfloat16 [1536, 1536], P('dp', 'tensor'), may hold values from -0.15625 to 0.15625
- w_value: bfloat16 [1536, 1536], P('dp', 'tensor'), may hold values from -0.15625 to 0.15625
- w_forget: bfloat16 [1536, 24], P(None, 'tensor'), may hold values from -0.15625 to 0.15625
- forget_bias: float32 [24], P('tensor'), may hold values from -1 to 7
- w_output: bfloat16 [1536, 1536], P('tensor', 'dp'), may hold values from -0.625 to 0.625
- mlp_gain: bfloat16 [1536], P('dp'), may hold values from 0.5 to 1.5
- w_gate: bfloat16 [1536, 4096], P('dp', 'tensor'), may hold values from -0.15625 to 0.15625
- w_up: bfloat16 [1536, 4096], P('dp', 'tensor'), may hold values from -0.15625 to 0.15625
- w_down: bfloat16 [4096, 1536], P('tensor', 'dp'), may hold values from -0.09375 to 0.09375
- segment_ids: int32 [8, 1024], P('dp'), may hold values from 0 to 3, never falling along the last dimension, each value on 1 to 512 neighbouring positions
- cotangent: bfloat16 [8192, 1536], P(('dp', 'tensor')), may hold values from -6 to 6
Outputs:
- output: bfloat16 [8192, 1536], P(('dp', 'tensor'))
- input_grad: float32 [8192, 1536], P(('dp', 'tensor'))
- grad_attn_gain: float32 [1536], P('dp')
- grad_w_query: float32 [1536, 1536], P('dp', 'tensor')
- grad_w_key: float32 [1536, 1536], P('dp', 'tensor')
- grad_w_value: float32 [1536, 1536], P('dp', 'tensor')
- grad_w_forget: float32 [1536, 24], P(None, 'tensor')
- grad_forget_bias: float32 [24], P('tensor')
- grad_w_output: float32 [1536, 1536], P('tensor', 'dp')
- grad_mlp_gain: float32 [1536], P('dp')
- grad_w_gate: float32 [1536, 4096], P('dp', 'tensor')
- grad_w_up: float32 [1536, 4096], P('dp', 'tensor')
- grad_w_down: float32 [4096, 1536], P('tensor', 'dp')
Inputs may be any that keep to these rules, and one draw needn't show every extreme that they name: Each row of segment_ids numbers the documents of one sequence in order, never falling; a document has 1 to 512 tokens, and the longest of a row has exactly 512.
All inputs are finite; a program needn't handle non-finite values.
Results may differ from a plain program's by a relative error of at most 0.018.
Values may be sent and summed in bfloat16 or wider, within the bound.
No kernel may reach another device: no remote copies, remote signals or barrier semaphores. Data moves between devices by JAX's collectives and lax.ppermute only.
A program may use at most 128 MiB of HBM per device.

v0:
```python
from functools import reduce
import jax
import jax.numpy as jnp
from jax import lax
from jax.sharding import PartitionSpec as P

HEAD_DIM = 64
EPS = 1e-06


def norm_rows(value, gain):
    scale = lax.rsqrt(jnp.mean(value * value, axis=-1, keepdims=True) + EPS)
    return (value * scale * gain, scale)


def norm_back(value, scale, gain, grad):
    weighted = grad * gain
    inner = jnp.mean(weighted * value, axis=-1, keepdims=True)
    return scale * weighted - value * (scale * scale * scale) * inner


def right_product(left, right):
    return jnp.dot(left, right, preferred_element_type=jnp.float32)


def back_terms(pairs):
    terms = [
        jnp.einsum("se,de->sd", grad, weight, preferred_element_type=jnp.float32)
        for grad, weight in pairs
    ]
    return reduce(jnp.add, terms)


def pair_scores(query_pair, key_pair, cum_pair, seg_row, start, block):
    length = key_pair.shape[0]
    raw = jnp.einsum("qhd,khd->hqk", query_pair, key_pair, preferred_element_type=jnp.float32)
    cum_rows = lax.dynamic_slice_in_dim(cum_pair, start, block, 1)
    scores = raw * 0.125 + cum_rows[:, :, None] - cum_pair[:, None, :]
    positions = start + jnp.arange(block, dtype=jnp.int32)
    columns = jnp.arange(length, dtype=jnp.int32)
    seg_rows = lax.dynamic_slice_in_dim(seg_row, start, block, 0)
    allowed = (columns[None, :] <= positions[:, None]) & (seg_rows[:, None] == seg_row[None, :])
    return jnp.where(allowed[None], scores, -jnp.inf)


def pair_inputs(index, blocks, block, query, keys, values, cumul):
    length = query.shape[0]
    span = 2 * HEAD_DIM
    group = index // blocks
    start = index % blocks * block
    column = group * span
    query_pair = lax.dynamic_slice(query, (start, column), (block, span)).reshape(
        block, 2, HEAD_DIM
    )
    key_pair = lax.dynamic_slice_in_dim(keys, column, span, 1).reshape(length, 2, HEAD_DIM)
    value_pair = lax.dynamic_slice_in_dim(values, column, span, 1).reshape(length, 2, HEAD_DIM)
    cum_pair = lax.dynamic_slice_in_dim(cumul, group * 2, 2, 0)
    return (group, start, column, query_pair, key_pair, value_pair, cum_pair)


def attend(query, keys, values, cumul, seg_row):
    length = query.shape[0]
    heads = query.shape[1] // HEAD_DIM
    block = min(512, length)
    blocks = length // block
    span = 2 * HEAD_DIM

    def step(index, carry):
        mixed, log_total = carry
        group, start, column, query_pair, key_pair, value_pair, cum_pair = pair_inputs(
            index, blocks, block, query, keys, values, cumul
        )
        scores = pair_scores(query_pair, key_pair, cum_pair, seg_row, start, block)
        top = jnp.max(scores, axis=-1, keepdims=True)
        expd = jnp.exp(scores - top)
        total = jnp.sum(expd, axis=-1, keepdims=True)
        probs = (expd / total).astype(jnp.bfloat16)
        out = jnp.einsum("hqk,khd->qhd", probs, value_pair, preferred_element_type=jnp.float32)
        mixed = lax.dynamic_update_slice(
            mixed, out.astype(jnp.bfloat16).reshape(block, span), (start, column)
        )
        log_total = lax.dynamic_update_slice(
            log_total, (top + jnp.log(total))[:, :, 0], (group * 2, start)
        )
        return (mixed, log_total)

    start_state = (jnp.zeros_like(query), jnp.zeros((heads, length), jnp.float32))
    return lax.fori_loop(0, heads // 2 * blocks, step, start_state)


def attend_back(query, keys, values, cumul, seg_row, log_total, grad_mixed):
    length = query.shape[0]
    heads = query.shape[1] // HEAD_DIM
    block = min(512, length)
    blocks = length // block
    span = 2 * HEAD_DIM

    def step(index, carry):
        grad_query, grad_keys, grad_values, grad_cum = carry
        group, start, column, query_pair, key_pair, value_pair, cum_pair = pair_inputs(
            index, blocks, block, query, keys, values, cumul
        )
        grad_pair = lax.dynamic_slice(grad_mixed, (start, column), (block, span)).reshape(
            block, 2, HEAD_DIM
        )
        scores = pair_scores(query_pair, key_pair, cum_pair, seg_row, start, block)
        lse_rows = lax.dynamic_slice(log_total, (group * 2, start), (2, block))
        probs = jnp.exp(scores - lse_rows[:, :, None])
        grad_probs = jnp.einsum(
            "qhd,khd->hqk", grad_pair, value_pair, preferred_element_type=jnp.float32
        )
        inner = jnp.sum(probs * grad_probs, axis=-1, keepdims=True)
        grad_scores = probs * (grad_probs - inner)
        rounded = grad_scores.astype(jnp.bfloat16)
        part_query = (
            jnp.einsum("hqk,khd->qhd", rounded, key_pair, preferred_element_type=jnp.float32)
            * 0.125
        )
        part_keys = (
            jnp.einsum("hqk,qhd->khd", rounded, query_pair, preferred_element_type=jnp.float32)
            * 0.125
        )
        part_values = jnp.einsum(
            "hqk,qhd->khd",
            probs.astype(jnp.bfloat16),
            grad_pair,
            preferred_element_type=jnp.float32,
        )
        grad_query = lax.dynamic_update_slice(
            grad_query, part_query.reshape(block, span), (start, column)
        )
        strip_keys = lax.dynamic_slice_in_dim(grad_keys, column, span, 1) + part_keys.reshape(
            length, span
        )
        grad_keys = lax.dynamic_update_slice_in_dim(grad_keys, strip_keys, column, 1)
        strip_values = lax.dynamic_slice_in_dim(grad_values, column, span, 1) + part_values.reshape(
            length, span
        )
        grad_values = lax.dynamic_update_slice_in_dim(grad_values, strip_values, column, 1)
        cum_cols = lax.dynamic_slice_in_dim(grad_cum, group * 2, 2, 0) - jnp.sum(
            grad_scores, axis=1
        )
        grad_cum = lax.dynamic_update_slice_in_dim(grad_cum, cum_cols, group * 2, 0)
        cum_rows = lax.dynamic_slice(grad_cum, (group * 2, start), (2, block)) + jnp.sum(
            grad_scores, axis=-1
        )
        grad_cum = lax.dynamic_update_slice(grad_cum, cum_rows, (group * 2, start))
        return (grad_query, grad_keys, grad_values, grad_cum)

    zeros_wide = jnp.zeros(query.shape, jnp.float32)
    start_state = (zeros_wide, zeros_wide, zeros_wide, jnp.zeros((heads, length), jnp.float32))
    return lax.fori_loop(0, heads // 2 * blocks, step, start_state)


def per_device(
    block_input,
    attn_gain,
    w_query,
    w_key,
    w_value,
    w_forget,
    forget_bias,
    w_output,
    mlp_gain,
    w_gate,
    w_up,
    w_down,
    segment_ids,
    cotangent,
):
    width = block_input.shape[1]
    heads = w_forget.shape[1]
    query_full, key_full, value_full, output_full, gain_one = (
        lax.all_gather(w_query, "dp", axis=0, tiled=True),
        lax.all_gather(w_key, "dp", axis=0, tiled=True),
        lax.all_gather(w_value, "dp", axis=0, tiled=True),
        lax.all_gather(w_output, "dp", axis=1, tiled=True),
        lax.all_gather(attn_gain, "dp", axis=0, tiled=True),
    )
    gate_full, up_full, down_full, gain_two = (
        lax.all_gather(w_gate, "dp", axis=0, tiled=True),
        lax.all_gather(w_up, "dp", axis=0, tiled=True),
        lax.all_gather(w_down, "dp", axis=1, tiled=True),
        lax.all_gather(mlp_gain, "dp", axis=0, tiled=True),
    )
    resid = block_input.astype(jnp.float32)
    normed, first_scale = norm_rows(resid, gain_one.astype(jnp.float32))
    normed_all = lax.all_gather(normed.astype(jnp.bfloat16), "tensor", axis=0, tiled=True)
    query = jnp.dot(normed_all, query_full, preferred_element_type=jnp.float32).astype(jnp.bfloat16)
    keys = jnp.dot(normed_all, key_full, preferred_element_type=jnp.float32).astype(jnp.bfloat16)
    values = jnp.dot(normed_all, value_full, preferred_element_type=jnp.float32).astype(
        jnp.bfloat16
    )
    forget_logit = jnp.dot(normed_all, w_forget, preferred_element_type=jnp.float32) + forget_bias
    cumul = jnp.cumsum(jax.nn.log_sigmoid(forget_logit), axis=0).T
    seg_row = segment_ids[0]
    mixed, log_total = attend(query, keys, values, cumul, seg_row)
    attn_out = lax.psum_scatter(
        right_product(mixed, output_full), "tensor", scatter_dimension=0, tiled=True
    )
    hidden_res = resid + attn_out
    second, second_scale = norm_rows(hidden_res, gain_two.astype(jnp.float32))
    second_all = lax.all_gather(second.astype(jnp.bfloat16), "tensor", axis=0, tiled=True)
    gate = jnp.dot(second_all, gate_full, preferred_element_type=jnp.float32)
    upper = jnp.dot(second_all, up_full, preferred_element_type=jnp.float32)
    sigma = jax.nn.sigmoid(gate)
    swish = gate * sigma
    hidden = (swish * upper).astype(jnp.bfloat16)
    mlp_out = lax.psum_scatter(
        right_product(hidden, down_full).astype(jnp.bfloat16),
        "tensor",
        scatter_dimension=0,
        tiled=True,
    ).astype(jnp.float32)
    output = (hidden_res + mlp_out).astype(jnp.bfloat16)
    (
        query_full,
        key_full,
        value_full,
        output_full,
        gain_one,
        gate_full,
        up_full,
        down_full,
        gain_two,
    ) = (
        lax.all_gather(w_query, "dp", axis=0, tiled=True),
        lax.all_gather(w_key, "dp", axis=0, tiled=True),
        lax.all_gather(w_value, "dp", axis=0, tiled=True),
        lax.all_gather(w_output, "dp", axis=1, tiled=True),
        lax.all_gather(attn_gain, "dp", axis=0, tiled=True),
        lax.all_gather(w_gate, "dp", axis=0, tiled=True),
        lax.all_gather(w_up, "dp", axis=0, tiled=True),
        lax.all_gather(w_down, "dp", axis=1, tiled=True),
        lax.all_gather(mlp_gain, "dp", axis=0, tiled=True),
    )
    grad_out = cotangent.astype(jnp.float32)
    grad_all = lax.all_gather(cotangent, "tensor", axis=0, tiled=True)
    grad_hidden = (
        jnp.einsum("sd,fd->sf", grad_all, down_full, preferred_element_type=jnp.float32)
        .astype(jnp.bfloat16)
        .astype(jnp.float32)
    )
    grad_gate = (grad_hidden * upper * sigma * (1.0 + gate * (1.0 - sigma))).astype(jnp.bfloat16)
    grad_up = (grad_hidden * swish).astype(jnp.bfloat16)
    grad_down_w = jnp.einsum("sf,sd->fd", hidden, grad_all, preferred_element_type=jnp.float32)
    grad_gate_w = jnp.einsum("sd,sf->df", second_all, grad_gate, preferred_element_type=jnp.float32)
    grad_up_w = jnp.einsum("sd,sf->df", second_all, grad_up, preferred_element_type=jnp.float32)
    grad_second = lax.psum_scatter(
        back_terms(((grad_gate, gate_full), (grad_up, up_full))).astype(jnp.bfloat16),
        "tensor",
        scatter_dimension=0,
        tiled=True,
    ).astype(jnp.float32)
    gain_two_f = gain_two.astype(jnp.float32)
    grad_res = grad_out + norm_back(hidden_res, second_scale, gain_two_f, grad_second)
    gain_two_part = jnp.sum(grad_second * hidden_res * second_scale, axis=0)
    mlp_shards = (
        lax.psum_scatter(
            grad_gate_w.astype(jnp.bfloat16), "dp", scatter_dimension=0, tiled=True
        ).astype(jnp.float32),
        lax.psum_scatter(
            grad_up_w.astype(jnp.bfloat16), "dp", scatter_dimension=0, tiled=True
        ).astype(jnp.float32),
        lax.psum_scatter(
            grad_down_w.astype(jnp.bfloat16), "dp", scatter_dimension=1, tiled=True
        ).astype(jnp.float32),
    )
    grad_branch = grad_res.astype(jnp.bfloat16)
    branch_all = lax.all_gather(grad_branch, "tensor", axis=0, tiled=True)
    grad_mixed = jnp.einsum(
        "sd,ed->se", branch_all, output_full, preferred_element_type=jnp.float32
    ).astype(jnp.bfloat16)
    grad_output_w = jnp.einsum("se,sd->ed", mixed, branch_all, preferred_element_type=jnp.float32)
    grad_query, grad_keys, grad_values, grad_cum = attend_back(
        query, keys, values, cumul, seg_row, log_total, grad_mixed
    )
    grad_logf = jnp.flip(jnp.cumsum(jnp.flip(grad_cum.T, 0), axis=0), 0)
    grad_logit = grad_logf * jax.nn.sigmoid(-forget_logit)
    grad_bias = jnp.sum(grad_logit, axis=0)
    logit_low = grad_logit.astype(jnp.bfloat16)
    query_low = grad_query.astype(jnp.bfloat16)
    keys_low = grad_keys.astype(jnp.bfloat16)
    values_low = grad_values.astype(jnp.bfloat16)
    grad_query_w = jnp.einsum(
        "sd,se->de", normed_all, query_low, preferred_element_type=jnp.float32
    )
    grad_key_w = jnp.einsum("sd,se->de", normed_all, keys_low, preferred_element_type=jnp.float32)
    grad_value_w = jnp.einsum(
        "sd,se->de", normed_all, values_low, preferred_element_type=jnp.float32
    )
    grad_forget_w = jnp.einsum(
        "sd,sh->dh", normed_all, logit_low, preferred_element_type=jnp.float32
    )
    grad_first = lax.psum_scatter(
        back_terms(
            (
                (query_low, query_full),
                (keys_low, key_full),
                (values_low, value_full),
                (logit_low, w_forget),
            )
        ).astype(jnp.bfloat16),
        "tensor",
        scatter_dimension=0,
        tiled=True,
    ).astype(jnp.float32)
    gain_one_f = gain_one.astype(jnp.float32)
    input_grad = grad_res + norm_back(resid, first_scale, gain_one_f, grad_first)
    gain_one_part = jnp.sum(grad_first * resid * first_scale, axis=0)
    attn_shards = (
        lax.psum_scatter(
            grad_query_w.astype(jnp.bfloat16), "dp", scatter_dimension=0, tiled=True
        ).astype(jnp.float32),
        lax.psum_scatter(
            grad_key_w.astype(jnp.bfloat16), "dp", scatter_dimension=0, tiled=True
        ).astype(jnp.float32),
        lax.psum_scatter(
            grad_value_w.astype(jnp.bfloat16), "dp", scatter_dimension=0, tiled=True
        ).astype(jnp.float32),
        lax.psum_scatter(
            grad_output_w.astype(jnp.bfloat16), "dp", scatter_dimension=1, tiled=True
        ).astype(jnp.float32),
    )
    tensor_index = lax.axis_index("tensor")
    all_heads = heads * lax.axis_size("tensor")
    forget_pad = lax.dynamic_update_slice(
        jnp.zeros((width, all_heads), jnp.float32), grad_forget_w, (0, tensor_index * heads)
    )
    bias_pad = lax.dynamic_update_slice(
        jnp.zeros((all_heads,), jnp.float32), grad_bias, (tensor_index * heads,)
    )
    summed = lax.psum((forget_pad, bias_pad, gain_one_part, gain_two_part), ("dp", "tensor"))
    share = width // lax.axis_size("dp")
    dp_start = lax.axis_index("dp") * share
    grad_forget_out = lax.dynamic_slice_in_dim(summed[0], tensor_index * heads, heads, 1)
    grad_bias_out = lax.dynamic_slice_in_dim(summed[1], tensor_index * heads, heads, 0)
    grad_gain_one = lax.dynamic_slice_in_dim(summed[2], dp_start, share, 0)
    grad_gain_two = lax.dynamic_slice_in_dim(summed[3], dp_start, share, 0)
    return (
        output,
        input_grad,
        grad_gain_one,
        attn_shards[0],
        attn_shards[1],
        attn_shards[2],
        grad_forget_out,
        grad_bias_out,
        attn_shards[3],
        grad_gain_two,
        mlp_shards[0],
        mlp_shards[1],
        mlp_shards[2],
    )


def solution(mesh):
    return jax.shard_map(
        per_device,
        mesh=mesh,
        in_specs=(
            P(("dp", "tensor"), None),
            P("dp"),
            P("dp", "tensor"),
            P("dp", "tensor"),
            P("dp", "tensor"),
            P(None, "tensor"),
            P("tensor"),
            P("tensor", "dp"),
            P("dp"),
            P("dp", "tensor"),
            P("dp", "tensor"),
            P("tensor", "dp"),
            P("dp", None),
            P(("dp", "tensor"), None),
        ),
        out_specs=(
            P(("dp", "tensor"), None),
            P(("dp", "tensor"), None),
            P("dp"),
            P("dp", "tensor"),
            P("dp", "tensor"),
            P("dp", "tensor"),
            P(None, "tensor"),
            P("tensor"),
            P("tensor", "dp"),
            P("dp"),
            P("dp", "tensor"),
            P("dp", "tensor"),
            P("tensor", "dp"),
        ),
        check_vma=False,
    )
```

profile of v0, /device:TPU:0, one launch (start us, length us, event | category | flops | bytes accessed | tf_op | source)
XLA Modules:
  0.0 1310.2 jit_solution(17133466086450550335)
XLA Ops:
  12.8 15.4 %all-reduce.3 = (bf16[1536]{0:T(1024)(128)(2,1)S(1)}, bf16[1536]{0:T(1024)(128)(2,1)S(1)}) all-reduce(bf16[1536]{0:T(1024)(128)(2,1)S(1)} %dynamic-update-slice, bf16[1536]{0:T(1024)(128)(2,1)S(1)} %dynamic-update-slice.1), channel_id=1, replica_groups=mesh['dp'=8,'tensor'=4] {'dp'}, use_global_device_ids=true, to_apply=%add | all-reduce | flops 3072 | bytes 12288
  33.9 60.3 %all-gather.12.cloned.1.call-done = bf16[1024,1536]{1,0:T(8,128)(2,1)} async-done(((bf16[256,1536]{1,0:T(8,128)(2,1)}), bf16[1024,1536]{1,0:T(8,128)(2,1)}) %all-gather.12.cloned.1.call-update) | async-done | bytes 3145744 | tf_op jit(solution)/shard_map/all_gather | solution.py:188
  99.9 18.9 %all-gather.18.cloned.1.call-done = bf16[1536,384]{1,0:T(8,128)(2,1)} async-done(((bf16[192,384]{1,0:T(8,128)(2,1)}), bf16[1536,384]{1,0:T(8,128)(2,1)}) %all-gather.18.cloned.1.call-update) | async-done | bytes 1179664 | tf_op jit(solution)/shard_map/all_gather | solution.py:175
  125.0 19.8 %all-gather.16.cloned.1.call-done = bf16[1536,384]{1,0:T(8,128)(2,1)} async-done(((bf16[192,384]{1,0:T(8,128)(2,1)}), bf16[1536,384]{1,0:T(8,128)(2,1)}) %all-gather.16.cloned.1.call-update) | async-done | bytes 1179664 | tf_op jit(solution)/shard_map/all_gather | solution.py:174
  151.0 19.6 %all-gather.14.cloned.1.call-done = bf16[1536,384]{1,0:T(8,128)(2,1)} async-done(((bf16[192,384]{1,0:T(8,128)(2,1)}), bf16[1536,384]{1,0:T(8,128)(2,1)}) %all-gather.14.cloned.1.call-update) | async-done | bytes 1179664 | tf_op jit(solution)/shard_map/all_gather | solution.py:176
  176.1 59.4 %while.40 = (s32[]{:T(128)}, bf16[1024,384]{0,1:T(8,128)(2,1)S(1)}, f32[6,1024]{1,0:T(8,128)S(1)}, bf16[1024,384]{0,1:T(8,128)(2,1)S(1)}, s32[1024]{0:T(1024)S(1...) while((s32[]{:T(128)}, bf16[1024,384]{0,1:T(8,128)(2,1)S(1)}, ...), condition=%wide.region_6.7_spmd, body=%wide.region_3.6_spmd.sunk | while | flops 288947744 | bytes 17148404 | solution.py:88
  244.4 108.4 %reduce-scatter.12.cloned.1.call-done = f32[256,1536]{1,0:T(8,128)} async-done(((f32[1024,1536]{1,0:T(8,128)}), f32[256,1536]{1,0:T(8,128)}) %reduce-scatter.12.cloned.1.call-update) | async-done | bytes 1572880 | tf_op jit(solution)/shard_map/reduce_scatter | solution.py:198
  356.4 62.0 %all-gather.30.cloned.1.call-done = bf16[1024,1536]{1,0:T(8,128)(2,1)} async-done(((bf16[256,1536]{1,0:T(8,128)(2,1)}), bf16[1024,1536]{1,0:T(8,128)(2,1)}) %all-gather.30.cloned.1.call-update) | async-done | bytes 3145744 | tf_op jit(solution)/shard_map/all_gather | solution.py:238
  418.4 32.9 %all-gather.28.cloned.1.call-done = bf16[1024,1536]{0,1:T(8,128)(2,1)} async-done(((bf16[1024,192]{0,1:T(8,128)(2,1)}), bf16[1024,1536]{0,1:T(8,128)(2,1)}) %all-gather.28.cloned.1.call-update) | async-done | bytes 3145744 | tf_op jit(solution)/shard_map/all_gather | solution.py:183
  458.9 26.6 %all-gather.24.cloned.1.call-done = bf16[1536,1024]{1,0:T(8,128)(2,1)} async-done(((bf16[192,1024]{1,0:T(8,128)(2,1)}), bf16[1536,1024]{1,0:T(8,128)(2,1)}) %all-gather.24.cloned.1.call-update) | async-done | bytes 3145744 | tf_op jit(solution)/shard_map/all_gather | solution.py:181
  485.5 65.5 %all-gather.22.cloned.1.call-done = bf16[1024,1536]{1,0:T(8,128)(2,1)} async-done(((bf16[256,1536]{1,0:T(8,128)(2,1)}), bf16[1024,1536]{1,0:T(8,128)(2,1)}) %all-gather.22.cloned.1.call-update) | async-done | bytes 3145744 | tf_op jit(solution)/shard_map/all_gather | solution.py:203
  559.3 24.7 %all-gather.26.cloned.1.call-done = bf16[1536,1024]{1,0:T(8,128)(2,1)} async-done(((bf16[192,1024]{1,0:T(8,128)(2,1)}), bf16[1536,1024]{1,0:T(8,128)(2,1)}) %all-gather.26.cloned.1.call-update) | async-done | bytes 3145744 | tf_op jit(solution)/shard_map/all_gather | solution.py:182
  583.9 10.9 fusion.14
  606.2 60.4 %reduce-scatter.16.cloned.1.call-done = bf16[256,1536]{1,0:T(8,128)(2,1)} async-done(((bf16[1024,1536]{1,0:T(8,128)(2,1)}), bf16[256,1536]{1,0:T(8,128)(2,1)}) %reduce-scatter.16.cloned.1.call-update) | async-done | bytes 786448 | tf_op jit(solution)/shard_map/reduce_scatter | solution.py:249
  697.2 37.8 %all-gather.32.cloned.1.call-done = bf16[1024,1536]{1,0:T(8,128)(2,1)} async-done(((bf16[256,1536]{1,0:T(8,128)(2,1)}), bf16[1024,1536]{1,0:T(8,128)(2,1)}) %all-gather.32.cloned.1.call-update) | async-done | bytes 3145744 | tf_op jit(solution)/shard_map/all_gather | solution.py:270
  741.1 91.9 %while.41 = (s32[]{:T(128)}, bf16[1024,384]{0,1:T(8,128)(2,1)}, f32[1024,384]{0,1:T(8,128)}, f32[1024,384]{0,1:T(8,128)S(1)}, f32[6,1024]{1,0:T(8,128)S(1)}, /*i...) while((s32[]{:T(128)}, bf16[1024,384]{0,1:T(8,128)(2,1)}, ...), condition=%wide.region_16.17_spmd, body=%wide.region_12.16_spmd.sunk | while | flops 686816768 | bytes 53156532 | solution.py:152
  885.5 124.8 %all-reduce.6.cloned.1.call-done = f32[1536,24]{0,1:T(8,128)} async-done(((f32[1536,24]{0,1:T(8,128)}), f32[1536,24]{0,1:T(8,128)}) %all-reduce.6.cloned.1.call-update) | async-done | bytes 147472 | tf_op jit(solution)/shard_map/psum | solution.py:333
  1011.8 40.7 %reduce-scatter.26.cloned.1.call-done = bf16[384,192]{0,1:T(8,128)(2,1)} async-done(((bf16[384,1536]{0,1:T(8,128)(2,1)}), bf16[384,192]{0,1:T(8,128)(2,1)}) %reduce-scatter.26.cloned.1.call-update) | async-done | bytes 147472 | tf_op jit(solution)/shard_map/reduce_scatter | solution.py:321
  1054.1 38.4 %reduce-scatter.20.cloned.1.call-done = bf16[192,384]{1,0:T(8,128)(2,1)} async-done(((bf16[1536,384]{1,0:T(8,128)(2,1)}), bf16[192,384]{1,0:T(8,128)(2,1)}) %reduce-scatter.20.cloned.1.call-update) | async-done | bytes 147472 | tf_op jit(solution)/shard_map/reduce_scatter | solution.py:312
  1094.1 38.6 %reduce-scatter.22.cloned.1.call-done = bf16[192,384]{1,0:T(8,128)(2,1)} async-done(((bf16[1536,384]{1,0:T(8,128)(2,1)}), bf16[192,384]{1,0:T(8,128)(2,1)}) %reduce-scatter.22.cloned.1.call-update) | async-done | bytes 147472 | tf_op jit(solution)/shard_map/reduce_scatter | solution.py:315
  1134.3 38.4 %reduce-scatter.24.cloned.1.call-done = bf16[192,384]{1,0:T(8,128)(2,1)} async-done(((bf16[1536,384]{1,0:T(8,128)(2,1)}), bf16[192,384]{1,0:T(8,128)(2,1)}) %reduce-scatter.24.cloned.1.call-update) | async-done | bytes 147472 | tf_op jit(solution)/shard_map/reduce_scatter | solution.py:318
  1174.4 61.0 %reduce-scatter.18.cloned.1.call-done = bf16[256,1536]{1,0:T(8,128)(2,1)} async-done(((bf16[1024,1536]{1,0:T(8,128)(2,1)}), bf16[256,1536]{1,0:T(8,128)(2,1)}) %reduce-scatter.18.cloned.1.call-update) | async-done | bytes 786448 | tf_op jit(solution)/shard_map/reduce_scatter | solution.py:295
  1237.1 45.5 %all-reduce.2 = (f32[1536]{0:T(1024)S(1)}, f32[24]{0:T(128)S(1)}, f32[1536]{0:T(1024)S(1)}) all-reduce(f32[1536]{0:T(1024)S(1)} %get-tuple-element.679, f32[24]{0:T(128)S(1)} %dynamic_update_slice.84, f32[1536]{0:T(1024)S(1)} %copy-done.25), channel_id=1, replica_groups=mesh['dp'=8,'tensor'=4] {'dp','tensor'}, use_global_device_ids=true, to_apply=%region_22.23 | all-reduce | flops 3096 | bytes 24768 | tf_op jit(solution)/shard_map/psum | solution.py:333
  1284.4 14.7 %reduce-scatter.14.cloned.1.call-done = bf16[256,1536]{1,0:T(8,128)(2,1)} async-done(((bf16[1024,1536]{1,0:T(8,128)(2,1)}), bf16[256,1536]{1,0:T(8,128)(2,1)}) %reduce-scatter.14.cloned.1.call-update) | async-done | bytes 786448 | tf_op jit(solution)/shard_map/reduce_scatter | solution.py:209
  (462 shorter events, 328.1 us)
Async XLA Ops:
  7.2 87.0 %all-gather.12.cloned.1.call-start = ((), (), s32[]{:S(2)}) async-start(), calls=%async_computation.11 | async-start | bytes 3932160 | tf_op jit(solution)/shard_map/all_gather | solution.py:188
  31.2 87.7 %all-gather.18.cloned.1.call-start = ((), (), s32[]{:S(2)}) async-start(), calls=%async_computation.14 | async-start | bytes 1327104 | tf_op jit(solution)/shard_map/all_gather | solution.py:175
  31.9 112.9 %all-gather.16.cloned.1.call-start = ((), (), s32[]{:S(2)}) async-start(), calls=%async_computation.13 | async-start | bytes 1327104 | tf_op jit(solution)/shard_map/all_gather | solution.py:174
  32.7 138.0 %all-gather.14.cloned.1.call-start = ((), (), s32[]{:S(2)}) async-start(), calls=%async_computation.12 | async-start | bytes 1327104 | tf_op jit(solution)/shard_map/all_gather | solution.py:176
  33.2 202.3 %all-gather.20.cloned.1.call-start = ((), (), s32[]{:S(2)}) async-start(), calls=%async_computation.15 | async-start | bytes 1327104 | tf_op jit(solution)/shard_map/all_gather | solution.py:177
  33.8 318.9 %reduce-scatter.12.cloned.1.call-start = ((), (), s32[]{:S(2)}) async-start(), calls=%async_computation.16 | async-start | bytes 7864320 | tf_op jit(solution)/shard_map/reduce_scatter | solution.py:198
  241.9 176.5 %all-gather.30.cloned.1.call-start = ((), (), s32[]{:S(2)}) async-start(), calls=%async_computation.22 | async-start | bytes 3932160 | tf_op jit(solution)/shard_map/all_gather | solution.py:238
  242.6 208.7 %all-gather.28.cloned.1.call-start = ((), (), s32[]{:S(2)}) async-start(), calls=%async_computation.20 | async-start | bytes 3538944 | tf_op jit(solution)/shard_map/all_gather | solution.py:183
  243.4 242.2 %all-gather.24.cloned.1.call-start = ((), (), s32[]{:S(2)}) async-start(), calls=%async_computation.18 | async-start | bytes 3538944 | tf_op jit(solution)/shard_map/all_gather | solution.py:181
  244.1 306.9 %all-gather.22.cloned.1.call-start = ((), (), s32[]{:S(2)}) async-start(), calls=%async_computation.17 | async-start | bytes 3932160 | tf_op jit(solution)/shard_map/all_gather | solution.py:203
  244.4 424.4 %copy-start.18 = (f32[1536]{0:T(1024)}, f32[1536]{0:T(1024)S(1)}, u32[]{:S(2)}) copy-start(f32[1536]{0:T(1024)S(1)} %convert_element_type.178) | copy-start | bytes 18436
  355.6 228.3 %all-gather.26.cloned.1.call-start = ((), (), s32[]{:S(2)}) async-start(), calls=%async_computation.19 | async-start | bytes 3538944 | tf_op jit(solution)/shard_map/all_gather | solution.py:182
  356.4 310.2 %reduce-scatter.16.cloned.1.call-start = ((), (), s32[]{:S(2)}) async-start(), calls=%async_computation.23 | async-start | bytes 3932160 | tf_op jit(solution)/shard_map/reduce_scatter | solution.py:249
  606.1 128.9 %all-gather.32.cloned.1.call-start = ((), (), s32[]{:S(2)}) async-start(), calls=%async_computation.24 | async-start | bytes 3932160 | tf_op jit(solution)/shard_map/all_gather | solution.py:270
  671.3 207.8 %reduce-scatter.30.cloned.1.call-start = ((), (), s32[]{:S(2)}) async-start(), calls=%async_computation.32 | async-start | bytes 3538944 | tf_op jit(solution)/shard_map/reduce_scatter | solution.py:262
  680.4 200.9 %reduce-scatter.28.cloned.1.call-start = ((), (), s32[]{:S(2)}) async-start(), calls=%async_computation.31 | async-start | bytes 3538944 | tf_op jit(solution)/shard_map/reduce_scatter | solution.py:259
  688.2 195.1 %reduce-scatter.32.cloned.1.call-start = ((), (), s32[]{:S(2)}) async-start(), calls=%async_computation.33 | async-start | bytes 3538944 | tf_op jit(solution)/shard_map/reduce_scatter | solution.py:265
  697.2 313.1 %all-reduce.6.cloned.1.call-start = ((), (), s32[]{:S(2)}) async-start(), calls=%async_computation.29 | async-start | bytes 294912 | tf_op jit(solution)/shard_map/psum | solution.py:333
  839.9 212.6 %reduce-scatter.26.cloned.1.call-start = ((), (), s32[]{:S(2)}) async-start(), calls=%async_computation.30 | async-start | bytes 1327104 | tf_op jit(solution)/shard_map/reduce_scatter | solution.py:321
  845.4 247.1 %reduce-scatter.20.cloned.1.call-start = ((), (), s32[]{:S(2)}) async-start(), calls=%async_computation.26 | async-start | bytes 1327104 | tf_op jit(solution)/shard_map/reduce_scatter | solution.py:312
  850.8 281.9 %reduce-scatter.22.cloned.1.call-start = ((), (), s32[]{:S(2)}) async-start(), calls=%async_computation.27 | async-start | bytes 1327104 | tf_op jit(solution)/shard_map/reduce_scatter | solution.py:315
  856.1 316.7 %reduce-scatter.24.cloned.1.call-start = ((), (), s32[]{:S(2)}) async-start(), calls=%async_computation.28 | async-start | bytes 1327104 | tf_op jit(solution)/shard_map/reduce_scatter | solution.py:318
  860.9 374.5 %reduce-scatter.18.cloned.1.call-start = ((), (), s32[]{:S(2)}) async-start(), calls=%async_computation.25 | async-start | bytes 3932160 | tf_op jit(solution)/shard_map/reduce_scatter | solution.py:295
  871.4 427.8 %reduce-scatter.14.cloned.1.call-start = ((), (), s32[]{:S(2)}) async-start(), calls=%async_computation.21 | async-start | bytes 3932160 | tf_op jit(solution)/shard_map/reduce_scatter | solution.py:209
  (65 other events, 5260.7 us)
Sparse Core Ops, SparseCore 0:
  31.3 62.8 all-gather.11
  96.1 22.6 all-gather.17
  120.7 24.0 all-gather.15
  146.5 24.0 all-gather.13
  172.4 24.0 all-gather.19
  242.0 110.7 reduce-scatter.11
  354.3 64.0 all-gather.29
  420.3 30.9 all-gather.27
  453.2 32.3 all-gather.23
  487.5 63.4 all-gather.21
  552.9 30.9 all-gather.25
  606.3 60.2 reduce-scatter.15
  671.5 63.5 all-gather.31
  738.3 44.9 reduce-scatter.29
  786.8 46.2 reduce-scatter.27
  836.3 46.3 reduce-scatter.31
  889.6 120.6 all-reduce.5
  1013.7 38.7 reduce-scatter.25
  1055.7 36.7 reduce-scatter.19
  1095.9 36.7 reduce-scatter.21
  1135.9 36.7 reduce-scatter.23
  1175.2 60.2 reduce-scatter.17
  1237.9 61.3 reduce-scatter.13
where the time goes:
time: 1320 us; the launch traced here: 1310 us
  waiting for transfers between devices  899 us (68%)
  matrix products  175 us (13%)
  local copies, waits for them, and re-layouts  96.2 us (7%)
  blocking collectives  61 us (5%)
  other arithmetic  60.4 us (5%)
  between operations  15.6 us (1%)
    psum x1, waiting for transfers between devices, per_device(): lax.psum((forget_pad, bias_pad, gain_one_part, gain_two_part), ('dp', 'te...  125 us
    reduce_scatter x1, waiting for transfers between devices, per_device(): lax.psum_scatter(right_product(mixed, output_full), 'tensor', scatter_dim...  108 us
    all_gather x1, waiting for transfers between devices, per_device(): lax.all_gather(second.astype(jnp.bfloat16), 'tensor', axis=0, tiled=True)  65.5 us
    all_gather x1, waiting for transfers between devices, per_device(): grad_all = lax.all_gather(cotangent, 'tensor', axis=0, tiled=True)  62 us
    reduce_scatter x1, waiting for transfers between devices, per_device(): lax.psum_scatter(back_terms(((query_low, query_full), (keys_low, key_full...  61 us
    reduce_scatter x1, waiting for transfers between devices, per_device(): lax.psum_scatter(back_terms(((grad_gate, gate_full), (grad_up, up_full)))...  60.4 us
    all_gather x1, waiting for transfers between devices, per_device(): lax.all_gather(normed.astype(jnp.bfloat16), 'tensor', axis=0, tiled=True)  60.3 us
    psum x1, blocking collectives, per_device(): lax.psum((forget_pad, bias_pad, gain_one_part, gain_two_part), ('dp', 'te...  45.5 us
  transfers between devices with their start and end apart: 23, of which 19 were waited for; matrix products, arithmetic and copies ran while one was open for 21% of the time, Pallas kernels for 0%

commit v1 on v0

--- a/solution.py
+++ b/solution.py
@@ -330,7 +330,9 @@
     bias_pad = lax.dynamic_update_slice(
         jnp.zeros((all_heads,), jnp.float32), grad_bias, (tensor_index * heads,)
     )
-    summed = lax.psum((forget_pad, bias_pad, gain_one_part, gain_two_part), ("dp", "tensor"))
+    summed = lax.psum(
+        lax.psum((forget_pad, bias_pad, gain_one_part, gain_two_part), "tensor"), "dp"
+    )
     share = width // lax.axis_size("dp")
     dp_start = lax.axis_index("dp") * share
     grad_forget_out = lax.dynamic_slice_in_dim(summed[0], tensor_index * heads, heads, 1)

time: 1320 us -> 1380 us (1.045)
  waiting for transfers between devices: 899 us -> 972 us
    psum x1 -> x2, waiting for transfers between devices: 125 us -> 61.1 us  [the longest x1 52.8 us: per_device(): lax.psum(lax.psum((forget_pad, bias_pad, gain_one_part, gain_two_part), '...]
    reduce_scatter x1, waiting for transfers between devices: 0.01 us -> 47.9 us  [per_device(): lax.psum_scatter(grad_down_w.astype(jnp.bfloat16), 'dp', scatter_dimensio...]
    reduce_scatter x1, waiting for transfers between devices: 0.02 us -> 47.5 us  [per_device(): lax.psum_scatter(grad_gate_w.astype(jnp.bfloat16), 'dp', scatter_dimensio...]
    all_gather x1, waiting for transfers between devices: 37.8 us -> 62.6 us  [per_device(): branch_all = lax.all_gather(grad_branch, 'tensor', axis=0, tiled=True)]
    psum x1 -> x2, blocking collectives: 45.5 us -> 41.7 us  [the longest x1 23.4 us: per_device(): lax.psum(lax.psum((forget_pad, bias_pad, gain_one_part, gain_two_part), '...]
  transfers between devices with their start and end apart: 23 -> 24, of which waited for: 19 -> 23; matrix products, arithmetic and copies ran while one was open for 21% -> 12% of each run, Pallas kernels for 0% -> 0%
where the time goes in v1:
time: 1380 us; the launch traced here: 1370 us
  waiting for transfers between devices  972 us (70%)
  matrix products  176 us (13%)
  local copies, waits for them, and re-layouts  83.3 us (6%)
  other arithmetic  60.4 us (4%)
  blocking collectives  57.1 us (4%)
  between operations  16 us (1%)
    reduce_scatter x1, waiting for transfers between devices, per_device(): lax.psum_scatter(right_product(mixed, output_full), 'tensor', scatter_dim...  108 us
    all_gather x1, waiting for transfers between devices, per_device(): lax.all_gather(second.astype(jnp.bfloat16), 'tensor', axis=0, tiled=True)  65.5 us
    all_gather x1, waiting for transfers between devices, per_device(): branch_all = lax.all_gather(grad_branch, 'tensor', axis=0, tiled=True)  62.6 us
    all_gather x1, waiting for transfers between devices, per_device(): grad_all = lax.all_gather(cotangent, 'tensor', axis=0, tiled=True)  62 us
    reduce_scatter x1, waiting for transfers between devices, per_device(): lax.psum_scatter(back_terms(((query_low, query_full), (keys_low, key_full...  61 us
    reduce_scatter x1, waiting for transfers between devices, per_device(): lax.psum_scatter(back_terms(((grad_gate, gate_full), (grad_up, up_full)))...  60.4 us
    all_gather x1, waiting for transfers between devices, per_device(): lax.all_gather(normed.astype(jnp.bfloat16), 'tensor', axis=0, tiled=True)  60.3 us
    psum x1, waiting for transfers between devices, per_device(): lax.psum(lax.psum((forget_pad, bias_pad, gain_one_part, gain_two_part), '...  52.8 us
  transfers between devices with their start and end apart: 24, of which 23 were waited for; matrix products, arithmetic and copies ran while one was open for 12% of the time, Pallas kernels for 0%

profile of v1, /device:TPU:0, one launch (start us, length us, event | category | flops | bytes accessed | tf_op | source)
XLA Modules:
  0.0 1367.8 jit_solution(2650914501283626880)
XLA Ops:
  33.3 60.3 %all-gather.12.cloned.1.call-done = bf16[1024,1536]{1,0:T(8,128)(2,1)} async-done(((bf16[256,1536]{1,0:T(8,128)(2,1)}), bf16[1024,1536]{1,0:T(8,128)(2,1)}) %all-gather.12.cloned.1.call-update) | async-done | bytes 3145744 | tf_op jit(solution)/shard_map/all_gather | solution.py:188
  98.6 19.6 %all-gather.18.cloned.1.call-done = bf16[1536,384]{1,0:T(8,128)(2,1)} async-done(((bf16[192,384]{1,0:T(8,128)(2,1)}), bf16[1536,384]{1,0:T(8,128)(2,1)}) %all-gather.18.cloned.1.call-update) | async-done | bytes 1179664 | tf_op jit(solution)/shard_map/all_gather | solution.py:175
  122.6 21.7 %all-gather.16.cloned.1.call-done = bf16[1536,384]{1,0:T(8,128)(2,1)} async-done(((bf16[192,384]{1,0:T(8,128)(2,1)}), bf16[1536,384]{1,0:T(8,128)(2,1)}) %all-gather.16.cloned.1.call-update) | async-done | bytes 1179664 | tf_op jit(solution)/shard_map/all_gather | solution.py:174
  148.5 21.5 %all-gather.14.cloned.1.call-done = bf16[1536,384]{1,0:T(8,128)(2,1)} async-done(((bf16[192,384]{1,0:T(8,128)(2,1)}), bf16[1536,384]{1,0:T(8,128)(2,1)}) %all-gather.14.cloned.1.call-update) | async-done | bytes 1179664 | tf_op jit(solution)/shard_map/all_gather | solution.py:176
  175.4 51.8 %while.40 = (s32[]{:T(128)}, bf16[1024,384]{0,1:T(8,128)(2,1)}, f32[6,1024]{1,0:T(8,128)S(1)}, bf16[1024,384]{0,1:T(8,128)(2,1)S(1)}, s32[1024]{0:T(1024)S(1)}, ...) while((s32[]{:T(128)}, bf16[1024,384]{0,1:T(8,128)(2,1)}, ...), condition=%wide.region_6.7_spmd, body=%wide.region_3.6_spmd.sunk | while | flops 288947744 | bytes 17148404 | solution.py:88
  236.6 108.4 %reduce-scatter.12.cloned.1.call-done = f32[256,1536]{1,0:T(8,128)} async-done(((f32[1024,1536]{1,0:T(8,128)}), f32[256,1536]{1,0:T(8,128)}) %reduce-scatter.12.cloned.1.call-update) | async-done | bytes 1572880 | tf_op jit(solution)/shard_map/reduce_scatter | solution.py:198
  348.6 62.0 %all-gather.30.cloned.1.call-done = bf16[1024,1536]{1,0:T(8,128)(2,1)} async-done(((bf16[256,1536]{1,0:T(8,128)(2,1)}), bf16[1024,1536]{1,0:T(8,128)(2,1)}) %all-gather.30.cloned.1.call-update) | async-done | bytes 3145744 | tf_op jit(solution)/shard_map/all_gather | solution.py:238
  410.6 32.9 %all-gather.28.cloned.1.call-done = bf16[1024,1536]{0,1:T(8,128)(2,1)} async-done(((bf16[1024,192]{0,1:T(8,128)(2,1)}), bf16[1024,1536]{0,1:T(8,128)(2,1)}) %all-gather.28.cloned.1.call-update) | async-done | bytes 3145744 | tf_op jit(solution)/shard_map/all_gather | solution.py:183
  451.1 26.6 %all-gather.24.cloned.1.call-done = bf16[1536,1024]{1,0:T(8,128)(2,1)} async-done(((bf16[192,1024]{1,0:T(8,128)(2,1)}), bf16[1536,1024]{1,0:T(8,128)(2,1)}) %all-gather.24.cloned.1.call-update) | async-done | bytes 3145744 | tf_op jit(solution)/shard_map/all_gather | solution.py:181
  477.8 65.5 %all-gather.22.cloned.1.call-done = bf16[1024,1536]{1,0:T(8,128)(2,1)} async-done(((bf16[256,1536]{1,0:T(8,128)(2,1)}), bf16[1024,1536]{1,0:T(8,128)(2,1)}) %all-gather.22.cloned.1.call-update) | async-done | bytes 3145744 | tf_op jit(solution)/shard_map/all_gather | solution.py:203
  551.5 24.7 %all-gather.26.cloned.1.call-done = bf16[1536,1024]{1,0:T(8,128)(2,1)} async-done(((bf16[192,1024]{1,0:T(8,128)(2,1)}), bf16[1536,1024]{1,0:T(8,128)(2,1)}) %all-gather.26.cloned.1.call-update) | async-done | bytes 3145744 | tf_op jit(solution)/shard_map/all_gather | solution.py:182
  598.5 60.4 %reduce-scatter.16.cloned.1.call-done = bf16[256,1536]{1,0:T(8,128)(2,1)} async-done(((bf16[1024,1536]{1,0:T(8,128)(2,1)}), bf16[256,1536]{1,0:T(8,128)(2,1)}) %reduce-scatter.16.cloned.1.call-update) | async-done | bytes 786448 | tf_op jit(solution)/shard_map/reduce_scatter | solution.py:249
  664.7 62.6 %all-gather.32.cloned.1.call-done = bf16[1024,1536]{1,0:T(8,128)(2,1)} async-done(((bf16[256,1536]{1,0:T(8,128)(2,1)}), bf16[1024,1536]{1,0:T(8,128)(2,1)}) %all-gather.32.cloned.1.call-update) | async-done | bytes 3145744 | tf_op jit(solution)/shard_map/all_gather | solution.py:270
  733.7 91.7 %while.41 = (s32[]{:T(128)}, bf16[1024,384]{0,1:T(8,128)(2,1)}, f32[1024,384]{0,1:T(8,128)}, f32[1024,384]{0,1:T(8,128)S(1)}, f32[6,1024]{1,0:T(8,128)S(1)}, /*i...) while((s32[]{:T(128)}, bf16[1024,384]{0,1:T(8,128)(2,1)}, ...), condition=%wide.region_16.17_spmd, body=%wide.region_12.16_spmd.sunk | while | flops 686816768 | bytes 53156532 | solution.py:152
  917.3 47.5 %reduce-scatter.28.cloned.1.call-done = bf16[192,1024]{1,0:T(8,128)(2,1)} async-done(((bf16[1536,1024]{1,0:T(8,128)(2,1)}), bf16[192,1024]{1,0:T(8,128)(2,1)}) %reduce-scatter.28.cloned.1.call-update) | async-done | bytes 393232 | tf_op jit(solution)/shard_map/reduce_scatter | solution.py:259
  966.8 47.9 %reduce-scatter.32.cloned.1.call-done = bf16[1024,192]{0,1:T(8,128)(2,1)} async-done(((bf16[1024,1536]{0,1:T(8,128)(2,1)}), bf16[1024,192]{0,1:T(8,128)(2,1)}) %reduce-scatter.32.cloned.1.call-update) | async-done | bytes 393232 | tf_op jit(solution)/shard_map/reduce_scatter | solution.py:265
  1016.9 52.8 %all-reduce.10.cloned.1.call-done = f32[1536,24]{0,1:T(8,128)} async-done(((f32[1536,24]{0,1:T(8,128)}), f32[1536,24]{0,1:T(8,128)}) %all-reduce.10.cloned.1.call-update) | async-done | bytes 147472 | tf_op jit(solution)/shard_map/psum | solution.py:333
  1071.1 39.3 %reduce-scatter.26.cloned.1.call-done = bf16[384,192]{0,1:T(8,128)(2,1)} async-done(((bf16[384,1536]{0,1:T(8,128)(2,1)}), bf16[384,192]{0,1:T(8,128)(2,1)}) %reduce-scatter.26.cloned.1.call-update) | async-done | bytes 147472 | tf_op jit(solution)/shard_map/reduce_scatter | solution.py:321
  1112.1 38.6 %reduce-scatter.20.cloned.1.call-done = bf16[192,384]{1,0:T(8,128)(2,1)} async-done(((bf16[1536,384]{1,0:T(8,128)(2,1)}), bf16[192,384]{1,0:T(8,128)(2,1)}) %reduce-scatter.20.cloned.1.call-update) | async-done | bytes 147472 | tf_op jit(solution)/shard_map/reduce_scatter | solution.py:312
  1152.3 38.4 %reduce-scatter.22.cloned.1.call-done = bf16[192,384]{1,0:T(8,128)(2,1)} async-done(((bf16[1536,384]{1,0:T(8,128)(2,1)}), bf16[192,384]{1,0:T(8,128)(2,1)}) %reduce-scatter.22.cloned.1.call-update) | async-done | bytes 147472 | tf_op jit(solution)/shard_map/reduce_scatter | solution.py:315
  1192.3 38.7 %reduce-scatter.24.cloned.1.call-done = bf16[192,384]{1,0:T(8,128)(2,1)} async-done(((bf16[1536,384]{1,0:T(8,128)(2,1)}), bf16[192,384]{1,0:T(8,128)(2,1)}) %reduce-scatter.24.cloned.1.call-update) | async-done | bytes 147472 | tf_op jit(solution)/shard_map/reduce_scatter | solution.py:318
  1232.7 61.0 %reduce-scatter.18.cloned.1.call-done = bf16[256,1536]{1,0:T(8,128)(2,1)} async-done(((bf16[1024,1536]{1,0:T(8,128)(2,1)}), bf16[256,1536]{1,0:T(8,128)(2,1)}) %reduce-scatter.18.cloned.1.call-update) | async-done | bytes 786448 | tf_op jit(solution)/shard_map/reduce_scatter | solution.py:295
  1295.3 18.3 %all-reduce.3 = (f32[1536]{0:T(1024)S(1)}, f32[24]{0:T(128)S(1)}, f32[1536]{0:T(1024)S(1)}) all-reduce(f32[1536]{0:T(1024)S(1)} %get-tuple-element.679, f32[24]{0:T(128)S(1)} %dynamic_update_slice.84, f32[1536]{0:T(1024)S(1)} %copy-done.24), channel_id=1, replica_groups=mesh['dp'=8,'tensor'=4] {'tensor'}, use_global_device_ids=true, to_apply=%region_22.23 | all-reduce | flops 3096 | bytes 24768 | tf_op jit(solution)/shard_map/psum | solution.py:334
  1313.6 23.4 %all-reduce.2 = (f32[1536]{0:T(1024)S(1)}, f32[24]{0:T(128)S(1)}, f32[1536]{0:T(1024)S(1)}) all-reduce(f32[1536]{0:T(1024)S(1)} %get-tuple-element.728, f32[24]{0:T(128)S(1)} %get-tuple-element.729, f32[1536]{0:T(1024)S(1)} %get-tuple-element.730), channel_id=1, replica_groups=mesh['dp'=8,'tensor'=4] {'dp'}, use_global_device_ids=true, to_apply=%region_23.24 | all-reduce | flops 3096 | bytes 24768 | tf_op jit(solution)/shard_map/psum | solution.py:333
  (464 shorter events, 378.7 us)
Async XLA Ops:
  7.2 86.4 %all-gather.12.cloned.1.call-start = ((), (), s32[]{:S(2)}) async-start(), calls=%async_computation.11 | async-start | bytes 3932160 | tf_op jit(solution)/shard_map/all_gather | solution.py:188
  30.6 87.7 %all-gather.18.cloned.1.call-start = ((), (), s32[]{:S(2)}) async-start(), calls=%async_computation.14 | async-start | bytes 1327104 | tf_op jit(solution)/shard_map/all_gather | solution.py:175
  31.3 112.9 %all-gather.16.cloned.1.call-start = ((), (), s32[]{:S(2)}) async-start(), calls=%async_computation.13 | async-start | bytes 1327104 | tf_op jit(solution)/shard_map/all_gather | solution.py:174
  32.1 138.0 %all-gather.14.cloned.1.call-start = ((), (), s32[]{:S(2)}) async-start(), calls=%async_computation.12 | async-start | bytes 1327104 | tf_op jit(solution)/shard_map/all_gather | solution.py:176
  32.7 194.6 %all-gather.20.cloned.1.call-start = ((), (), s32[]{:S(2)}) async-start(), calls=%async_computation.15 | async-start | bytes 1327104 | tf_op jit(solution)/shard_map/all_gather | solution.py:177
  33.2 311.8 %reduce-scatter.12.cloned.1.call-start = ((), (), s32[]{:S(2)}) async-start(), calls=%async_computation.16 | async-start | bytes 7864320 | tf_op jit(solution)/shard_map/reduce_scatter | solution.py:198
  234.1 176.5 %all-gather.30.cloned.1.call-start = ((), (), s32[]{:S(2)}) async-start(), calls=%async_computation.22 | async-start | bytes 3932160 | tf_op jit(solution)/shard_map/all_gather | solution.py:238
  234.9 208.7 %all-gather.28.cloned.1.call-start = ((), (), s32[]{:S(2)}) async-start(), calls=%async_computation.20 | async-start | bytes 3538944 | tf_op jit(solution)/shard_map/all_gather | solution.py:183
  235.6 242.2 %all-gather.24.cloned.1.call-start = ((), (), s32[]{:S(2)}) async-start(), calls=%async_computation.18 | async-start | bytes 3538944 | tf_op jit(solution)/shard_map/all_gather | solution.py:181
  236.3 306.9 %all-gather.22.cloned.1.call-start = ((), (), s32[]{:S(2)}) async-start(), calls=%async_computation.17 | async-start | bytes 3932160 | tf_op jit(solution)/shard_map/all_gather | solution.py:203
  347.9 228.3 %all-gather.26.cloned.1.call-start = ((), (), s32[]{:S(2)}) async-start(), calls=%async_computation.19 | async-start | bytes 3538944 | tf_op jit(solution)/shard_map/all_gather | solution.py:182
  348.6 310.2 %reduce-scatter.16.cloned.1.call-start = ((), (), s32[]{:S(2)}) async-start(), calls=%async_computation.23 | async-start | bytes 3932160 | tf_op jit(solution)/shard_map/reduce_scatter | solution.py:249
  598.4 128.9 %all-gather.32.cloned.1.call-start = ((), (), s32[]{:S(2)}) async-start(), calls=%async_computation.24 | async-start | bytes 3932160 | tf_op jit(solution)/shard_map/all_gather | solution.py:270
  663.6 201.8 %all-reduce.8.cloned.1.call-start = ((), (), s32[]{:S(2)}) async-start(), calls=%async_computation.29 | async-start | bytes 294912 | tf_op jit(solution)/shard_map/psum | solution.py:334
  832.3 83.0 %reduce-scatter.30.cloned.1.call-start = ((), (), s32[]{:S(2)}) async-start(), calls=%async_computation.33 | async-start | bytes 3538944 | tf_op jit(solution)/shard_map/reduce_scatter | solution.py:262
  841.6 123.3 %reduce-scatter.28.cloned.1.call-start = ((), (), s32[]{:S(2)}) async-start(), calls=%async_computation.32 | async-start | bytes 3538944 | tf_op jit(solution)/shard_map/reduce_scatter | solution.py:259
  849.3 165.4 %reduce-scatter.32.cloned.1.call-start = ((), (), s32[]{:S(2)}) async-start(), calls=%async_computation.34 | async-start | bytes 3538944 | tf_op jit(solution)/shard_map/reduce_scatter | solution.py:265
  857.0 212.6 %all-reduce.10.cloned.1.call-start = ((), (), s32[]{:S(2)}) async-start(), calls=%async_computation.30 | async-start | bytes 294912 | tf_op jit(solution)/shard_map/psum | solution.py:333
  865.5 245.0 %reduce-scatter.26.cloned.1.call-start = ((), (), s32[]{:S(2)}) async-start(), calls=%async_computation.31 | async-start | bytes 1327104 | tf_op jit(solution)/shard_map/reduce_scatter | solution.py:321
  870.8 279.9 %reduce-scatter.20.cloned.1.call-start = ((), (), s32[]{:S(2)}) async-start(), calls=%async_computation.26 | async-start | bytes 1327104 | tf_op jit(solution)/shard_map/reduce_scatter | solution.py:312
  875.8 314.9 %reduce-scatter.22.cloned.1.call-start = ((), (), s32[]{:S(2)}) async-start(), calls=%async_computation.27 | async-start | bytes 1327104 | tf_op jit(solution)/shard_map/reduce_scatter | solution.py:315
  881.5 349.6 %reduce-scatter.24.cloned.1.call-start = ((), (), s32[]{:S(2)}) async-start(), calls=%async_computation.28 | async-start | bytes 1327104 | tf_op jit(solution)/shard_map/reduce_scatter | solution.py:318
  886.5 407.2 %reduce-scatter.18.cloned.1.call-start = ((), (), s32[]{:S(2)}) async-start(), calls=%async_computation.25 | async-start | bytes 3932160 | tf_op jit(solution)/shard_map/reduce_scatter | solution.py:295
  897.0 459.4 %reduce-scatter.14.cloned.1.call-start = ((), (), s32[]{:S(2)}) async-start(), calls=%async_computation.21 | async-start | bytes 3932160 | tf_op jit(solution)/shard_map/reduce_scatter | solution.py:209
  (65 other events, 5962.4 us)
Sparse Core Ops, SparseCore 0:
  30.7 62.8 all-gather.11
  95.5 22.6 all-gather.17
  120.1 24.0 all-gather.15
  146.0 24.0 all-gather.13
  171.8 24.0 all-gather.19
  234.2 110.7 reduce-scatter.11
  346.6 64.0 all-gather.29
  412.5 30.9 all-gather.27
  445.4 32.3 all-gather.23
  479.8 63.4 all-gather.21
  545.2 30.9 all-gather.25
  598.5 60.2 reduce-scatter.15
  663.8 63.5 all-gather.31
  832.5 32.9 all-reduce.7
  869.1 46.2 reduce-scatter.29
  918.6 46.2 reduce-scatter.27
  968.5 46.1 reduce-scatter.31
  1017.7 51.9 all-reduce.9
  1072.8 37.5 reduce-scatter.25
  1113.9 36.7 reduce-scatter.19
  1153.9 36.7 reduce-scatter.21
  1194.3 36.7 reduce-scatter.23
  1233.4 60.2 reduce-scatter.17
  1295.8 60.5 reduce-scatter.13
